TPU v7x, 512 devices: a whole 4x4x16 slice. The times are simulated.
512 devices in a mesh: ctx: 64 (over x, z), head: 8 (over y, core).
Axes of the slice: x: 4, y: 4, z: 16, core: 2. Of those that a mesh axis runs over, the one named last changes fastest.
Arguments:
- queries: bfloat16 [65536, 4096], P('ctx', 'head'), may hold values from -8 to 8
- span_key_array: bfloat16 [65536, 1024], P('ctx', 'head'), may hold values from -8 to 8
- span_value_array: bfloat16 [65536, 1024], P('ctx', 'head'), may hold values from -6 to 6
- cached_key_array: bfloat16 [262144, 1024], P('ctx', 'head'), may hold values from -8 to 8
- cached_value_array: bfloat16 [262144, 1024], P('ctx', 'head'), may hold values from -6 to 6
- chosen: int32 [128, 8, 3], P('ctx', 'head'), may hold values from 0 to 511, as said below
Outputs:
- attended: bfloat16 [65536, 4096], P(('ctx', 'head'))
Inputs may be any that keep to these rules, and one draw needn't show every extreme that they name: For each query block and KV head the 3 numbers are cache blocks on 3 different devices (block b lies on index b // 8 of ctx). For one KV head, over all query blocks, at most 2 of the 8 blocks of one device are ever chosen, and exactly 2 on some device.
All inputs are finite; a program needn't handle non-finite values.
Results may differ from a plain program's by a relative error of at most 0.0049.
Values may be sent and summed in bfloat16 or wider, within the bound.
A program may use at most 64 MiB of HBM per device.

v0:
```python
import math

import jax
import jax.numpy as jnp
from jax import lax
from jax.sharding import PartitionSpec as P

HEAD_SIZE = 128
BLOCK_TOKENS = 512
CHOSEN_COUNT = 3


def shortened(value):
    return jax.tree.map(lambda a: a.astype(jnp.bfloat16) if a.dtype == jnp.float32 else a, value)


def dot_rows(left, right):
    return lax.dot_general(
        left, right, (((1,), (1,)), ((), ())), preferred_element_type=jnp.float32
    )


def shards(queries, span_key_array, span_value_array, cached_key_array, cached_value_array, chosen):
    peer_count = lax.axis_size("ctx")
    row_count, q_width = queries.shape
    kv_width = span_key_array.shape[1]
    kv_local = kv_width // HEAD_SIZE
    group_share = q_width // kv_width
    blocks_dev = cached_key_array.shape[0] // BLOCK_TOKENS
    q_blocks = row_count // BLOCK_TOKENS
    slice_len = BLOCK_TOKENS // peer_count
    everyone = lax.all_gather(chosen, "ctx", axis=0, tiled=True)
    wanted = everyone.reshape(peer_count, q_blocks, kv_local, CHOSEN_COUNT)
    shaped_keys = cached_key_array.reshape(blocks_dev, peer_count, slice_len, kv_width)
    shaped_values = cached_value_array.reshape(blocks_dev, peer_count, slice_len, kv_width)
    held_keys, held_values = (
        lax.all_to_all(shaped_keys, "ctx", split_axis=1, concat_axis=0, tiled=True),
        lax.all_to_all(shaped_values, "ctx", split_axis=1, concat_axis=0, tiled=True),
    )
    held_keys = held_keys.reshape(peer_count * blocks_dev, slice_len, kv_local, HEAD_SIZE)
    held_values = held_values.reshape(peer_count * blocks_dev, slice_len, kv_local, HEAD_SIZE)
    key_tables = held_keys[:, :, 0, :]
    value_tables = held_values[:, :, 0, :]
    positions = wanted[:, :, 0, :]
    sent_keys = jnp.stack([jnp.take(key_tables, positions, axis=0)], axis=2)
    sent_values = jnp.stack([jnp.take(value_tables, positions, axis=0)], axis=2)
    got_keys, got_values = (
        lax.all_to_all(sent_keys, "ctx", split_axis=0, concat_axis=4, tiled=True),
        lax.all_to_all(sent_values, "ctx", split_axis=0, concat_axis=4, tiled=True),
    )
    distant_keys = got_keys.reshape(q_blocks, kv_local, CHOSEN_COUNT * BLOCK_TOKENS, HEAD_SIZE)
    distant_values = got_values.reshape(q_blocks, kv_local, CHOSEN_COUNT * BLOCK_TOKENS, HEAD_SIZE)
    inv_root = 1.0 / math.sqrt(HEAD_SIZE)
    causal = jnp.arange(BLOCK_TOKENS)[:, None] >= jnp.arange(BLOCK_TOKENS)[None, :]
    visible = jnp.concatenate(
        [causal, jnp.ones((BLOCK_TOKENS, CHOSEN_COUNT * BLOCK_TOKENS), dtype=bool)], axis=1
    )

    def one_block(inputs):
        block_queries, block_keys, block_values, block_far_keys, block_far_values = inputs
        results = []
        all_keys = jnp.concatenate([block_keys, block_far_keys[0]], axis=0)
        all_values = jnp.concatenate([block_values, block_far_values[0]], axis=0)
        for q_head in range(group_share):
            head_queries = block_queries[:, q_head * HEAD_SIZE : (q_head + 1) * HEAD_SIZE]
            scores = dot_rows(head_queries, all_keys) * inv_root
            scores = jnp.where(visible, scores, -jnp.inf)
            row_max = jnp.max(scores, axis=1, keepdims=True)
            exponent = jnp.exp(scores - row_max)
            weights = (exponent / jnp.sum(exponent, axis=1, keepdims=True)).astype(jnp.bfloat16)
            results.append(
                jnp.dot(weights, all_values, preferred_element_type=jnp.float32).astype(
                    jnp.bfloat16
                )
            )
        return jnp.concatenate(results, axis=1)

    attended = lax.map(
        one_block,
        (
            queries.reshape(q_blocks, BLOCK_TOKENS, q_width),
            span_key_array.reshape(q_blocks, BLOCK_TOKENS, kv_width),
            span_value_array.reshape(q_blocks, BLOCK_TOKENS, kv_width),
            distant_keys,
            distant_values,
        ),
    )
    attended = attended.reshape(row_count, q_width)
    return lax.all_to_all(
        shortened(attended), "head", split_axis=0, concat_axis=1, tiled=True
    ).astype(attended.dtype)


def solution(mesh):
    placed = (
        P("ctx", "head"),
        P("ctx", "head"),
        P("ctx", "head"),
        P("ctx", "head"),
        P("ctx", "head"),
        P("ctx", "head", None),
    )
    return jax.shard_map(
        shards, mesh=mesh, in_specs=placed, out_specs=P(("ctx", "head"), None), check_vma=False
    )
```

profile of v0, /device:TPU:1, one launch (start us, length us, event | category | flops | bytes accessed | tf_op | source)
XLA Modules:
  0.0 341.4 jit_solution(10843265766982345700)
XLA Ops:
  0.0 0.0 copy-start
  0.0 0.0 copy-start.1
  0.0 2.6 copy.19
  2.6 19.1 %all-to-all-start = ((bf16[8,64,8,128]{3,2,0,1:T(8,128)(2,1)}), bf16[8,64,8,128]{3,2,0,1:T(8,128)(2,1)S(1)}, u32[]{:S(2)}, u32[]{:S(2)}) async-start(bf16[8,64,8,128]{3,2,0,1:T(8,128)(2,1)} %copy.19), calls=%async_computation | async-start | bytes 2097152 | tf_op jit(solution)/shard_map/all_to_all | solution.py:37
  21.7 0.0 copy-done
  21.7 1.3 copy.22
  23.0 49.0 %all-to-all-done = bf16[8,64,8,128]{3,2,0,1:T(8,128)(2,1)S(1)} async-done(((bf16[8,64,8,128]{3,2,0,1:T(8,128)(2,1)}), bf16[8,64,8,128]{3,2,0,1:T(8,128)(2,1)S(1)}, u32[]{:S(2)}, u32[]{:S(2)}) %all-to-all-start) | async-done | bytes 1048608 | tf_op jit(solution)/shard_map/all_to_all | solution.py:37
  72.0 10.1 %all-to-all-start.2 = ((bf16[8,64,8,128]{3,2,0,1:T(8,128)(2,1)}), bf16[8,64,8,128]{3,2,0,1:T(8,128)(2,1)S(1)}, u32[]{:S(2)}, u32[]{:S(2)}) async-start(bf16[8,64,8,128]{3,2,0,1:T(8,128)(2,1)} %copy.22), calls=%async_computation.2 | async-start | bytes 2097152 | tf_op jit(solution)/shard_map/all_to_all | solution.py:38
  82.2 0.0 copy-done.1
  82.2 103.0 %all_gather.3 = s32[128,1,3]{2,1,0:T(1,128)S(1)} all-gather(s32[2,1,3]{2,1,0:T(1,128)S(1)} %copy-done.1), channel_id=1, replica_groups=mesh['ctx'=64,'head'=8] {'ctx'}, dimensions={0}, use_global_device_ids=true | all-gather | bytes 1560 | tf_op jit(solution)/shard_map/all_gather | solution.py:32
  185.2 0.2 reshape.72
  185.4 0.1 compare_and_fusion
  185.5 1.7 gather_fusion
  187.3 0.0 all-to-all-done.2
  187.3 1.7 gather_fusion.1
  189.0 1.3 select_bitcast_fusion
  190.4 36.7 %all_to_all.79 = bf16[64,2,1,3,8,128]{5,4,3,1,2,0:T(8,128)(2,1)S(1)} all-to-all(bf16[64,2,1,3,8,128]{5,4,3,1,2,0:T(8,128)(2,1)S(1)} %get-tuple-element.94), channel_id=1, replica_groups=mesh['ctx'=64,'head'=8] {'ctx'}, dimensions={0} | all-to-all | bytes 1572864 | tf_op jit(solution)/shard_map/all_to_all | solution.py:48
  227.0 7.7 %all-to-all-start.3 = ((bf16[64,2,1,3,8,128]{5,4,3,1,2,0:T(8,128)(2,1)}), bf16[64,2,1,3,8,128]{5,4,3,1,2,0:T(8,128)(2,1)S(1)}, u32[]{:S(2)}, u32[]{:S(2)}) async-start(bf16[64,2,1,3,8,128]{5,4,3,1,2,0:T(8,128)(2,1)} %get-tuple-element.93), calls=%async_computation.3 | async-start | bytes 1572864 | tf_op jit(solution)/shard_map/all_to_all | solution.py:49
  234.8 0.1 iota_compare_fusion
  234.9 0.9 concatenate.12
  235.7 0.1 copy.21
  235.9 28.0 %all-to-all-done.3 = bf16[64,2,1,3,8,128]{5,4,3,1,2,0:T(8,128)(2,1)S(1)} async-done(((bf16[64,2,1,3,8,128]{5,4,3,1,2,0:T(8,128)(2,1)}), bf16[64,2,1,3,8,128]{5,4,3,1,2,0:T(8,128)(2,1)S(1)}, u32[]{:S(2)}, u32[]{:S(2)}) %all-to-all-start.3) | async-done | bytes 786464 | tf_op jit(solution)/shard_map/all_to_all | solution.py:49
  263.9 1.0 copy.24
  264.9 31.0 %while.10 = (s32[]{:T(128)}, bf16[2,512,512]{2,1,0:T(8,128)(2,1)}, bf16[2,512,512]{2,1,0:T(8,128)(2,1)}, bf16[2,512,128]{2,1,0:T(8,128)(2,1)}, bf16[2,1,1536,128...) while((s32[]{:T(128)}, bf16[2,512,512]{2,1,0:T(8,128)(2,1)}, ...), condition=%wide.region_9.11_spmd, body=%wide.region_0.10_spmd.sunk | while | flops 2191781888 | bytes 66101864 | solution.py:78
  264.9 1.0 dynamic-slice_bitcast_fusion.8
  266.0 1.0 dynamic-slice_bitcast_fusion.9
  266.9 1.1 dynamic-slice_bitcast_fusion.10
  268.0 0.9 fusion.41
  269.0 0.7 fusion.42
  269.7 1.1 fusion.43
  270.8 0.9 fusion.38
  271.8 0.7 fusion.39
  272.5 1.1 fusion.40
  273.7 0.9 fusion.35
  274.6 0.7 fusion.36
  275.3 1.1 fusion.37
  276.5 0.9 fusion.32
  277.4 0.7 fusion.33
  278.1 1.1 fusion.34
  279.3 0.2 copy.33
  279.5 0.8 constant_dynamic-update-slice_fusion.2
  280.4 1.0 dynamic-slice_bitcast_fusion.8
  281.4 1.0 dynamic-slice_bitcast_fusion.9
  282.4 1.1 dynamic-slice_bitcast_fusion.10
  283.5 0.9 fusion.41
  284.5 0.7 fusion.42
  285.2 1.1 fusion.43
  286.3 0.9 fusion.38
  287.3 0.7 fusion.39
  288.0 1.1 fusion.40
  289.1 0.9 fusion.35
  290.1 0.7 fusion.36
  290.8 1.1 fusion.37
  292.0 0.9 fusion.32
  292.9 0.7 fusion.33
  293.6 1.1 fusion.34
  294.8 0.2 copy.33
  295.0 0.8 constant_dynamic-update-slice_fusion.2
  295.9 43.6 %all_to_all.80 = bf16[8,128,512]{2,1,0:T(8,128)(2,1)S(1)} all-to-all(bf16[8,128,512]{2,1,0:T(8,128)(2,1)} %bitcast.74), channel_id=1, replica_groups=mesh['ctx'=64,'head'=8] {'head'}, dimensions={0} | all-to-all | bytes 2097152 | tf_op jit(solution)/shard_map/all_to_all | solution.py:89
  339.4 0.7 copy.28
  340.1 1.3 copy.29
  (5 shorter events, 0.1 us)
Async XLA Ops:
  0.0 21.7 %copy-start = (bf16[4096,128]{1,0:T(8,128)(2,1)S(1)}, bf16[4096,128]{1,0:T(8,128)(2,1)}, u32[]{:S(2)}) copy-start(bf16[4096,128]{1,0:T(8,128)(2,1)} %param.14) | copy-start | bytes 3145732
  0.0 82.2 %copy-start.1 = (s32[2,1,3]{2,1,0:T(1,128)S(1)}, s32[2,1,3]{2,1,0:T(1,128)}, u32[]{:S(2)}) copy-start(s32[2,1,3]{2,1,0:T(1,128)} %param.15) | copy-start | bytes 76
  2.6 69.4 %all-to-all-start = ((bf16[8,64,8,128]{3,2,0,1:T(8,128)(2,1)}), bf16[8,64,8,128]{3,2,0,1:T(8,128)(2,1)S(1)}, u32[]{:S(2)}, u32[]{:S(2)}) async-start(bf16[8,64,8,128]{3,2,0,1:T(8,128)(2,1)} %copy.19), calls=%async_computation | async-start | bytes 2097152 | tf_op jit(solution)/shard_map/all_to_all | solution.py:37
  72.0 115.2 %all-to-all-start.2 = ((bf16[8,64,8,128]{3,2,0,1:T(8,128)(2,1)}), bf16[8,64,8,128]{3,2,0,1:T(8,128)(2,1)S(1)}, u32[]{:S(2)}, u32[]{:S(2)}) async-start(bf16[8,64,8,128]{3,2,0,1:T(8,128)(2,1)} %copy.22), calls=%async_computation.2 | async-start | bytes 2097152 | tf_op jit(solution)/shard_map/all_to_all | solution.py:38
  227.0 36.9 %all-to-all-start.3 = ((bf16[64,2,1,3,8,128]{5,4,3,1,2,0:T(8,128)(2,1)}), bf16[64,2,1,3,8,128]{5,4,3,1,2,0:T(8,128)(2,1)S(1)}, u32[]{:S(2)}, u32[]{:S(2)}) async-start(bf16[64,2,1,3,8,128]{5,4,3,1,2,0:T(8,128)(2,1)} %get-tuple-element.93), calls=%async_computation.3 | async-start | bytes 1572864 | tf_op jit(solution)/shard_map/all_to_all | solution.py:49
where the time goes:
time: 342 us; the launch traced here: 341 us
  blocking collectives  183 us (54%)
  waiting for transfers between devices  77.1 us (23%)
  starting transfers between devices  37 us (11%)
  local copies, waits for them, and re-layouts  19.9 us (6%)
  matrix products  16.7 us (5%)
  other arithmetic  7.29 us (2%)
    all_gather x1, blocking collectives, shards(): everyone = lax.all_gather(chosen, 'ctx', axis=0, tiled=True)  103 us
    all_to_all x1, waiting for transfers between devices, shards(): lax.all_to_all(shaped_keys, 'ctx', split_axis=1, concat_axis=0, tiled=True)  49 us
    all_to_all x1, blocking collectives, shards(): lax.all_to_all(shortened(attended), 'head', split_axis=0, concat_axis=1,...  43.6 us
    all_to_all x1, blocking collectives, shards(): lax.all_to_all(sent_keys, 'ctx', split_axis=0, concat_axis=4, tiled=True)  36.7 us
    all_to_all x1, waiting for transfers between devices, shards(): lax.all_to_all(sent_values, 'ctx', split_axis=0, concat_axis=4, tiled=True)  28 us
    all_to_all x1, starting transfers between devices, shards(): lax.all_to_all(shaped_keys, 'ctx', split_axis=1, concat_axis=0, tiled=True)  19.1 us
    all_to_all x1, starting transfers between devices, shards(): lax.all_to_all(shaped_values, 'ctx', split_axis=1, concat_axis=0, tiled=T...  10.1 us
    dot_general x8, matrix products, one_block(): jnp.dot(weights, all_values, preferred_element_type=jnp.float32)  9.18 us
  transfers between devices with their start and end apart: 3, of which 2 were waited for; matrix products, arithmetic and copies ran while one was open for 1% of the time, Pallas kernels for 0%

commit v1 on v0

v1 whole, which is shorter than its diff:
```python
import functools
import math

import jax
import jax.numpy as jnp
from jax import lax
from jax.experimental import pallas as pl
from jax.experimental.pallas import tpu as pltpu
from jax.sharding import PartitionSpec as P

HEAD_SIZE = 128
BLOCK = 512
PICKS = 3
HOT = 2
NX, NZ = 4, 16
HALF = NZ // 2
REACH = HALF // 2
N_CTX = NX * NZ
N_HEAD = 8
SLICES = NX * HALF
ROWS = BLOCK // SLICES
GROUP = 4
Q_BLOCKS = 2
DEV_BLOCKS = 8
LIST = BLOCK * (PICKS + 1)
CHUNK = 256
LOG2_SCALE = math.log2(math.e) / math.sqrt(HEAD_SIZE)
BIG = 1 << 20
MESH = pl.DeviceIdType.MESH


def dot_rows(left, right):
    return lax.dot_general(
        left, right, (((1,), (1,)), ((), ())), preferred_element_type=jnp.float32
    )


def remote(src, dst, send_sem, recv_sem, axis, peer):
    return pltpu.make_async_remote_copy(
        src_ref=src,
        dst_ref=dst,
        send_sem=send_sem,
        recv_sem=recv_sem,
        device_id={axis: peer},
        device_id_type=MESH,
    )


def drain(ref, sem):
    pltpu.make_async_copy(ref, ref, sem).wait()


def kernel(
    q_hbm, ks_hbm, vs_hbm, kc_hbm, vc_hbm, chosen_ref, out_hbm,
    q_v, ks_v, vs_v, cache_k, cache_w, hot_v, table_k, table_w, send_v, far_v,
    row_v, all_v, index_v, index_s, weights_v, out_v,
    load_sem, index_sem, ch_send, ch_recv, p1_send, p1_recv, p2_send, p2_recv,
    out_send, out_recv, out_local,
):
    me = lax.axis_index("ctx")
    head = lax.axis_index("head")
    mx, mz = me // NZ, me % NZ
    place = mx * HALF + mz % HALF
    caches, tables = (cache_k, cache_w), (table_k, table_w)

    loads = [
        pltpu.make_async_copy(kc_hbm, cache_k, load_sem.at[0]),
        pltpu.make_async_copy(vc_hbm, cache_w, load_sem.at[1]),
        pltpu.make_async_copy(q_hbm, q_v, load_sem.at[2]),
        pltpu.make_async_copy(ks_hbm, ks_v, load_sem.at[3]),
        pltpu.make_async_copy(vs_hbm, vs_v, load_sem.at[4]),
    ]
    for load in loads:
        load.start()

    barrier = pltpu.get_barrier_semaphore()

    @pl.loop(1, N_CTX)
    def _(i):
        pl.semaphore_signal(
            barrier, inc=1, device_id={"ctx": (me + i) % N_CTX}, device_id_type=MESH
        )

    @pl.loop(1, N_HEAD)
    def _(i):
        pl.semaphore_signal(
            barrier, inc=1, device_id={"head": (head + i) % N_HEAD}, device_id_type=MESH
        )

    lane = lax.broadcasted_iota(jnp.int32, (1, 128), 1)
    mine = jnp.full((1, 128), -1, jnp.int32)
    for b in range(Q_BLOCKS):
        for j in range(PICKS):
            mine = jnp.where(lane == b * PICKS + j, chosen_ref[b, 0, j], mine)
    row_v[0] = mine
    pl.semaphore_wait(barrier, N_CTX - 1 + N_HEAD - 1)

    @pl.loop(1, N_CTX)
    def _(i):
        remote(row_v.at[0], all_v.at[me], ch_send, ch_recv, "ctx", (me + i) % N_CTX).start()

    all_v[me] = mine
    drain(all_v.at[pl.ds(0, N_CTX - 1)], ch_recv)
    picked = all_v[...].reshape(N_CTX, 128)
    owner = jnp.where(picked < 0, -1, picked // DEV_BLOCKS)
    here = owner == me
    low = jnp.min(jnp.where(here, picked, BIG))
    high = jnp.max(jnp.where(here, picked, -1))
    first = me * DEV_BLOCKS
    low = jnp.clip(low - first, 0, DEV_BLOCKS - 1)
    high = jnp.clip(high - first, 0, DEV_BLOCKS - 1)

    def spread(t):
        loads[t].wait()
        hot_v[t, 0] = caches[t][low]
        hot_v[t, 1] = caches[t][high]

        @pl.loop(1, N_CTX)
        def _(i):
            x = (mx + i // NZ) % NX
            z = (mz + i * 5) % NZ
            at = pl.multiple_of((x * HALF + z % HALF) * ROWS, ROWS)
            remote(
                hot_v.at[t, :, pl.ds(at, ROWS)],
                tables[t].at[pl.ds(me * HOT, HOT)],
                p1_send.at[t], p1_recv.at[t], "ctx", x * NZ + z,
            ).start()

        at = pl.multiple_of(place * ROWS, ROWS)
        tables[t][pl.ds(me * HOT, HOT)] = hot_v[t, :, pl.ds(at, ROWS)]

    spread(0)
    spread(1)

    lane_c = lax.broadcasted_iota(jnp.int32, (N_CTX, 128), 1)
    lows = jnp.full((1, 128), BIG, jnp.int32)
    for e in range(Q_BLOCKS * PICKS):
        hit = owner[:, e : e + 1] == lane_c
        lows = jnp.minimum(
            lows, jnp.min(jnp.where(hit, picked[:, e : e + 1], BIG), axis=0, keepdims=True)
        )
    index = jnp.zeros((N_CTX, 128), jnp.int32)
    for e in range(Q_BLOCKS * PICKS):
        hit = owner[:, e : e + 1] == lane_c
        least = jnp.min(jnp.where(hit, lows, BIG), axis=1, keepdims=True)
        spot = owner[:, e : e + 1] * HOT + (picked[:, e : e + 1] != least).astype(jnp.int32)
        index = jnp.where(lane_c == e, spot, index)
    index_v[...] = index
    to_scalar = pltpu.make_async_copy(index_v, index_s, index_sem)
    to_scalar.start()
    to_scalar.wait()

    def fill(t, b, peer, ref):
        for j in range(PICKS):
            ref[pl.ds(j * ROWS, ROWS)] = tables[t][index_s[peer, b * PICKS + j]]

    def deliver(t, b):
        fill(t, b, me, far_v.at[t, b, place])
        stay = REACH - 1 + b

        @pl.loop(0, SLICES - 1)
        def _(i):
            i = i + jnp.where(i >= stay, 1, 0)
            x = (mx + i // HALF) % NX
            z = (mz + i % HALF - stay + NZ) % NZ
            peer = x * NZ + z
            fill(t, b, peer, send_v.at[t, b, i])
            remote(
                send_v.at[t, b, i], far_v.at[t, b, place],
                p2_send.at[t], p2_recv.at[t, b], "ctx", peer,
            ).start()

    def hold(t):
        drain(tables[t].at[pl.ds(0, HOT * (N_CTX - 1))], p1_recv.at[t])
        for b in range(Q_BLOCKS):
            deliver(t, b)

    hold(0)
    hold(1)
    for load in loads[2:]:
        load.wait()

    def softmax(b):
        drain(far_v.at[0, b, pl.ds(0, SLICES - 1)], p2_recv.at[0, b])
        far_keys = far_v[0, b].reshape(PICKS * BLOCK, HEAD_SIZE)

        @pl.loop(0, GROUP)
        def _(h):
            for r in range(BLOCK // CHUNK):
                query = q_v[
                    b * BLOCK + r * CHUNK : b * BLOCK + (r + 1) * CHUNK,
                    pl.ds(pl.multiple_of(h * HEAD_SIZE, HEAD_SIZE), HEAD_SIZE),
                ]
                near = dot_rows(query, ks_v[b * BLOCK : (b + 1) * BLOCK])
                below = (
                    r * CHUNK + lax.broadcasted_iota(jnp.int32, (CHUNK, BLOCK), 0)
                    >= lax.broadcasted_iota(jnp.int32, (CHUNK, BLOCK), 1)
                )
                near = jnp.where(below, near, -jnp.inf)
                far = dot_rows(query, far_keys)
                top = jnp.maximum(
                    jnp.max(near, axis=1, keepdims=True), jnp.max(far, axis=1, keepdims=True)
                )
                near = jnp.exp2((near - top) * LOG2_SCALE)
                far = jnp.exp2((far - top) * LOG2_SCALE)
                share = 1.0 / (
                    jnp.sum(near, axis=1, keepdims=True) + jnp.sum(far, axis=1, keepdims=True)
                )
                rows = pl.ds(r * CHUNK, CHUNK)
                weights_v[b, h, rows, 0:BLOCK] = (near * share).astype(jnp.bfloat16)
                weights_v[b, h, rows, BLOCK:LIST] = (far * share).astype(jnp.bfloat16)

    def combine(b):
        drain(far_v.at[1, b, pl.ds(0, SLICES - 1)], p2_recv.at[1, b])
        far_values = far_v[1, b].reshape(PICKS * BLOCK, HEAD_SIZE)
        near_values = vs_v[b * BLOCK : (b + 1) * BLOCK]

        @pl.loop(0, GROUP)
        def _(h):
            total = jnp.dot(
                weights_v[b, h, :, 0:BLOCK], near_values, preferred_element_type=jnp.float32
            ) + jnp.dot(
                weights_v[b, h, :, BLOCK:LIST], far_values, preferred_element_type=jnp.float32
            )
            out_v[
                pl.ds(b * BLOCK, BLOCK), pl.ds(pl.multiple_of(h * HEAD_SIZE, HEAD_SIZE), HEAD_SIZE)
            ] = total.astype(jnp.bfloat16)

        for t in range(b * GROUP, (b + 1) * GROUP):
            give(t, True)

    def give(t, start):
        width = GROUP * HEAD_SIZE
        part = out_v.at[pl.ds(t * 128, 128)]
        spot = out_hbm.at[:, pl.ds(pl.multiple_of(head * width, width), width)]

        @pl.when(t != head)
        def _():
            copy = remote(part, spot, out_send.at[t], out_recv, "head", t)
            if start:
                copy.start()
            else:
                copy.wait_send()

        @pl.when(t == head)
        def _():
            copy = pltpu.make_async_copy(part, spot, out_local)
            if start:
                copy.start()
            else:
                copy.wait()

    for b in range(Q_BLOCKS):
        softmax(b)
    for b in range(Q_BLOCKS):
        combine(b)
    drain(out_hbm.at[:, pl.ds(0, (N_HEAD - 1) * GROUP * HEAD_SIZE)], out_recv)
    for t in range(N_HEAD):
        give(t, False)
    drain(all_v.at[pl.ds(0, N_CTX - 1)], ch_send)
    for t in range(2):
        drain(tables[t].at[pl.ds(0, HOT * (N_CTX - 1))], p1_send.at[t])
        drain(send_v.at[t, :, pl.ds(0, SLICES - 1)], p2_send.at[t])


def shards(queries, span_keys, span_values, cached_keys, cached_values, chosen):
    rows, width = queries.shape
    bf16 = jnp.bfloat16
    anywhere = pl.BlockSpec(memory_space=pl.ANY)
    dma = pltpu.SemaphoreType.DMA
    return pl.pallas_call(
        kernel,
        out_shape=jax.ShapeDtypeStruct((rows // N_HEAD, width * N_HEAD), bf16),
        in_specs=[anywhere] * 5 + [pl.BlockSpec(memory_space=pltpu.SMEM)],
        out_specs=anywhere,
        scratch_shapes=[
            pltpu.VMEM((rows, width), bf16),
            pltpu.VMEM((rows, HEAD_SIZE), bf16),
            pltpu.VMEM((rows, HEAD_SIZE), bf16),
            pltpu.VMEM((DEV_BLOCKS, BLOCK, HEAD_SIZE), bf16),
            pltpu.VMEM((DEV_BLOCKS, BLOCK, HEAD_SIZE), bf16),
            pltpu.VMEM((2, HOT, BLOCK, HEAD_SIZE), bf16),
            pltpu.VMEM((HOT * N_CTX, ROWS, HEAD_SIZE), bf16),
            pltpu.VMEM((HOT * N_CTX, ROWS, HEAD_SIZE), bf16),
            pltpu.VMEM((2, Q_BLOCKS, SLICES, PICKS * ROWS, HEAD_SIZE), bf16),
            pltpu.VMEM((2, Q_BLOCKS, SLICES, PICKS * ROWS, HEAD_SIZE), bf16),
            pltpu.VMEM((1, 1, 128), jnp.int32),
            pltpu.VMEM((N_CTX, 1, 128), jnp.int32),
            pltpu.VMEM((N_CTX, 128), jnp.int32),
            pltpu.SMEM((N_CTX, 128), jnp.int32),
            pltpu.VMEM((Q_BLOCKS, GROUP, BLOCK, LIST), bf16),
            pltpu.VMEM((rows, width), bf16),
            dma((5,)), dma, dma, dma, dma((2,)), dma((2,)), dma((2,)), dma((2, 2)),
            dma((N_HEAD,)), dma, dma,
        ],
        compiler_params=pltpu.CompilerParams(
            collective_id=0, has_side_effects=True, vmem_limit_bytes=56 << 20
        ),
        cost_estimate=pl.CostEstimate(
            flops=4 * rows * GROUP * LIST * HEAD_SIZE,
            bytes_accessed=8 << 20,
            transcendentals=rows * GROUP * LIST,
        ),
    )(
        queries, span_keys, span_values,
        cached_keys.reshape(DEV_BLOCKS, BLOCK, HEAD_SIZE),
        cached_values.reshape(DEV_BLOCKS, BLOCK, HEAD_SIZE),
        chosen,
    )


def solution(mesh):
    placed = (P("ctx", "head"),) * 5 + (P("ctx", "head", None),)
    return jax.shard_map(
        shards, mesh=mesh, in_specs=placed, out_specs=P(("ctx", "head"), None), check_vma=False
    )
```

time: 342 us -> 124 us (0.36)
  blocking collectives: 183 us -> 0 us
  Pallas kernels: 0 us -> 120 us
  waiting for transfers between devices: 77.1 us -> 0 us
  starting transfers between devices: 37 us -> 0 us
  local copies, waits for them, and re-layouts: 19.9 us -> 2.29 us
  matrix products: 16.7 us -> 0 us
  other arithmetic: 7.29 us -> 0 us
    pallas_call x0 -> x1, Pallas kernels: none -> 120 us  [shards(): pl.pallas_call(kernel, out_shape=jax.ShapeDtypeStruct((rows // N_HEAD, wi...]
    all_gather x1 -> x0, blocking collectives: 103 us -> none  [shards(): everyone = lax.all_gather(chosen, 'ctx', axis=0, tiled=True)]
    all_to_all x2 -> x0, blocking collectives: 80.2 us -> none  [the longest x1 43.6 us: shards(): lax.all_to_all(shortened(attended), 'head', split_axis=0, concat_axis=1,...]
    all_to_all x3 -> x0, waiting for transfers between devices: 77.1 us -> none  [the longest x1 49 us: shards(): lax.all_to_all(shaped_keys, 'ctx', split_axis=1, concat_axis=0, tiled=True)]
    all_to_all x3 -> x0, starting transfers between devices: 37 us -> none  [the longest x1 19.1 us: shards(): lax.all_to_all(shaped_keys, 'ctx', split_axis=1, concat_axis=0, tiled=True)]
    dot_general x16 -> x0, matrix products: 16.7 us -> none  [the longest x8 9.18 us: one_block(): jnp.dot(weights, all_values, preferred_element_type=jnp.float32)]
    squeeze x6 -> x0, local copies, waits for them, and re-layouts: 6.24 us -> none  [the longest x4 4.15 us: shards(): lax.map(one_block, (queries.reshape(q_blocks, BLOCK_TOKENS, q_width), spa...]
    reduce_sum x8 -> x0, other arithmetic: 5.69 us -> none  [one_block(): jnp.sum(exponent, axis=1, keepdims=True)]
  transfers between devices with their start and end apart: 3 -> 0, of which waited for: 2 -> 0; matrix products, arithmetic and copies ran while one was open for 1% -> 0% of each run, Pallas kernels for 0% -> 0%
where the time goes in v1:
time: 124 us; the launch traced here: 122 us
  Pallas kernels  120 us (97%)
  local copies, waits for them, and re-layouts  2.29 us (2%)
    pallas_call x1, Pallas kernels, shards(): pl.pallas_call(kernel, out_shape=jax.ShapeDtypeStruct((rows // N_HEAD, wi...  120 us

profile of v1, /device:TPU:1, one launch (start us, length us, event | category | flops | bytes accessed | tf_op | source)
XLA Modules:
  0.0 122.4 jit_solution(1922220869451501216)
XLA Ops:
  0.0 120.1 %shard_map.64 = bf16[128,4096]{1,0:T(8,128)(2,1)} custom-call(bf16[1024,512]{1,0:T(8,128)(2,1)} %q_hbm.1, bf16[1024,128]{1,0:T(8,128)(2,1)} %ks_hbm.1, bf16[1024,128]{1,0:T(8,128)(2,1)} %vs_hbm.1, bf16[8,512,128]{2,1,0:T(8,128)(2,1)} %bitcast.2, bf16[8,512,128]{2,1,0:T(8,128)(2,1)} %bitcast.3, s32[2,1,3]{2,1,0:T(1,128)} %chosen_ref.1), custom_call_target="tpu_custom_call" | custom-call | flops 4294967296 | bytes 8388608 | tf_op jit(solution)/shard_map/pallas_call | solution.py:271
  120.1 2.3 %copy.8 = bf16[128,4096]{1,0:T(8,128)(2,1)} copy(bf16[128,4096]{1,0:T(8,128)(2,1)} %shard_map.64) | data formatting | bytes 2097152

commit v2 on v1

v2 whole, which is shorter than its diff:
```python
import functools
import math

import jax
import jax.numpy as jnp
from jax import lax
from jax.experimental import pallas as pl
from jax.experimental.pallas import tpu as pltpu
from jax.sharding import PartitionSpec as P

HEAD_SIZE = 128
BLOCK = 512
PICKS = 3
HOT = 2
NX, NZ = 4, 16
HALF = NZ // 2
FAR_X = (2, 1, 3)
REACH = HALF // 2
N_CTX = NX * NZ
N_HEAD = 8
SLICES = NX * HALF
ROWS = BLOCK // SLICES
COLUMN = BLOCK // NX
GROUP = 4
OWN_ROWS = 128
Q_BLOCKS = 2
DEV_BLOCKS = 8
LIST = BLOCK * (PICKS + 1)
CHUNK = 256
LOG2_SCALE = math.log2(math.e) / math.sqrt(HEAD_SIZE)
BIG = 1 << 20
MESH = pl.DeviceIdType.MESH


def dot_rows(left, right):
    return lax.dot_general(
        left, right, (((1,), (1,)), ((), ())), preferred_element_type=jnp.float32
    )


def remote(src, dst, send_sem, recv_sem, axis, peer):
    return pltpu.make_async_remote_copy(
        src_ref=src,
        dst_ref=dst,
        send_sem=send_sem,
        recv_sem=recv_sem,
        device_id={axis: peer},
        device_id_type=MESH,
    )


def drain(ref, sem):
    pltpu.make_async_copy(ref, ref, sem).wait()


def kernel(
    q_hbm, ks_hbm, vs_hbm, kc_hbm, vc_hbm, chosen_ref, out_ref,
    q_v, ks_v, vs_v, cache_k, cache_w, hot_v, column_v, table_k, table_w, send_v, relay_v, far_v,
    row_v, all_v, index_v, index_s, weights_v, out_v,
    load_sem, index_sem, ch_send, ch_recv, p1_send, p1_recv, p2_send, p2_recv,
    x1_recv, x2_recv, out_send, out_recv, out_local,
):
    me = lax.axis_index("ctx")
    head = lax.axis_index("head")
    mx, mz = me // NZ, me % NZ
    mine_at = mz % HALF
    caches, tables = (cache_k, cache_w), (table_k, table_w)

    def along_x(d):
        return (mx + d) % NX * NZ + mz

    def along_z(d):
        return mx * NZ + (mz + d) % NZ

    loads = [
        pltpu.make_async_copy(kc_hbm, cache_k, load_sem.at[0]),
        pltpu.make_async_copy(vc_hbm, cache_w, load_sem.at[1]),
        pltpu.make_async_copy(q_hbm, q_v, load_sem.at[2]),
        pltpu.make_async_copy(ks_hbm, ks_v, load_sem.at[3]),
        pltpu.make_async_copy(vs_hbm, vs_v, load_sem.at[4]),
    ]
    for load in loads[:2]:
        load.start()

    def far_first(i):
        return HALF + (i + 1) // 2 * (1 - i % 2 * 2)

    barrier = pltpu.get_barrier_semaphore()

    def greet(axis, peer):
        pl.semaphore_signal(barrier, inc=1, device_id={axis: peer}, device_id_type=MESH)

    @pl.loop(0, NZ - 1)
    def _(i):
        greet("ctx", along_z(far_first(i)))

    for d in FAR_X:
        greet("ctx", along_x(d))

    @pl.loop(1, N_HEAD)
    def _(i):
        greet("head", (head + i) % N_HEAD)

    lane = lax.broadcasted_iota(jnp.int32, (1, 128), 1)
    mine = jnp.full((1, 128), -1, jnp.int32)
    for b in range(Q_BLOCKS):
        for j in range(PICKS):
            mine = jnp.where(lane == b * PICKS + j, chosen_ref[b, 0, j], mine)
    row_v[0] = mine
    all_v[me] = mine
    pl.semaphore_wait(barrier, NZ - 1 + NX - 1 + N_HEAD - 1)

    @pl.loop(0, NZ - 1)
    def _(i):
        remote(
            row_v.at[0], all_v.at[me], ch_send.at[0], ch_recv.at[0], "ctx",
            along_z(far_first(i)),
        ).start()

    drain(all_v.at[pl.ds(0, NZ - 1)], ch_recv.at[0])
    column = all_v.at[pl.ds(mx * NZ, NZ)]

    for d in FAR_X:
        remote(column, column, ch_send.at[1], ch_recv.at[1], "ctx", along_x(d)).start()

    drain(all_v.at[pl.ds(0, (NX - 1) * NZ)], ch_recv.at[1])
    picked = all_v[...].reshape(N_CTX, 128)
    owner = jnp.where(picked < 0, -1, picked // DEV_BLOCKS)
    here = owner == me
    low = jnp.min(jnp.where(here, picked, BIG))
    high = jnp.max(jnp.where(here, picked, -1))
    first = me * DEV_BLOCKS
    low = jnp.clip(low - first, 0, DEV_BLOCKS - 1)
    high = jnp.clip(high - first, 0, DEV_BLOCKS - 1)

    def spread_x(t):
        loads[t].wait()
        hot_v[t, 0] = caches[t][low]
        hot_v[t, 1] = caches[t][high]
        for d in range(1, NX):
            at = pl.multiple_of((mx + d) % NX * COLUMN, COLUMN)
            remote(
                hot_v.at[t, :, pl.ds(at, COLUMN)],
                column_v.at[t, pl.ds((NX - d) * HOT, HOT)],
                p1_send.at[t], x1_recv.at[t], "ctx", along_x(d),
            ).start()
        at = pl.multiple_of(mx * COLUMN, COLUMN)
        column_v[t, 0:HOT] = hot_v[t, :, pl.ds(at, COLUMN)]

    def spread_z(t, start, count):
        @pl.loop(1, NZ)
        def _(i):
            at = pl.multiple_of((mz + i * 5) % HALF * ROWS, ROWS)
            remote(
                column_v.at[t, pl.ds(start, count), pl.ds(at, ROWS)],
                tables[t].at[pl.ds(mz * HOT * NX + start, count)],
                p1_send.at[t], p1_recv.at[t], "ctx", along_z(i * 5),
            ).start()

        at = pl.multiple_of(mine_at * ROWS, ROWS)
        tables[t][pl.ds(mz * HOT * NX + start, count)] = column_v[
            t, pl.ds(start, count), pl.ds(at, ROWS)
        ]

    spread_x(0)
    spread_z(0, 0, HOT)
    spread_x(1)
    drain(column_v.at[0, pl.ds(HOT, HOT * (NX - 1))], x1_recv.at[0])
    spread_z(0, HOT, HOT * (NX - 1))
    drain(column_v.at[1, pl.ds(HOT, HOT * (NX - 1))], x1_recv.at[1])
    spread_z(1, 0, HOT * NX)

    for load in loads[2:]:
        load.start()

    lane_c = lax.broadcasted_iota(jnp.int32, (N_CTX, 128), 1)
    lows = jnp.full((1, 128), BIG, jnp.int32)
    for e in range(Q_BLOCKS * PICKS):
        hit = owner[:, e : e + 1] == lane_c
        lows = jnp.minimum(
            lows, jnp.min(jnp.where(hit, picked[:, e : e + 1], BIG), axis=0, keepdims=True)
        )
    index = jnp.zeros((N_CTX, 128), jnp.int32)
    for e in range(Q_BLOCKS * PICKS):
        at = owner[:, e : e + 1]
        hit = at == lane_c
        least = jnp.min(jnp.where(hit, lows, BIG), axis=1, keepdims=True)
        later = (picked[:, e : e + 1] != least).astype(jnp.int32)
        spot = (at % NZ * NX + (at // NZ + NX - mx) % NX) * HOT + later
        index = jnp.where(lane_c == e, spot, index)
    index_v[...] = index
    to_scalar = pltpu.make_async_copy(index_v, index_s, index_sem)
    to_scalar.start()
    to_scalar.wait()

    def fill(t, b, peer, ref):
        for j in range(PICKS):
            ref[pl.ds(j * ROWS, ROWS)] = tables[t][index_s[peer, b * PICKS + j]]

    def z_shift(b, k):
        return k + NZ - (REACH - 1 + b)

    def deliver_x(t, b):
        @pl.loop(0, HALF)
        def _(k):
            fill(t, b, along_z(z_shift(b, k)), relay_v.at[t, b, 0, k])

        for d in range(1, NX):
            @pl.loop(0, HALF)
            def _(k):
                peer = (mx + d) % NX * NZ + (mz + z_shift(b, k)) % NZ
                fill(t, b, peer, send_v.at[t, b, d - 1, k])

            remote(
                send_v.at[t, b, d - 1], relay_v.at[t, b, NX - d],
                p2_send.at[t], x2_recv.at[t, b], "ctx", along_x(d),
            ).start()

    def deliver_z(t, b):
        drain(relay_v.at[t, b, pl.ds(1, NX - 1)], x2_recv.at[t, b])
        stay = REACH - 1 + b

        @pl.loop(0, HALF - 1)
        def _(i):
            k = (stay + 3 + i * 3) % HALF
            remote(
                relay_v.at[t, b, :, k], far_v.at[t, b, mine_at],
                p2_send.at[t], p2_recv.at[t, b], "ctx", along_z(z_shift(b, k)),
            ).start()

        far_v[t, b, mine_at] = relay_v[t, b, :, stay]

    lead = 1 - head // (N_HEAD // 2)
    order = (lead, 1 - lead)
    for t in range(2):
        drain(tables[t].at[pl.ds(0, HOT * NX * (NZ - 1))], p1_recv.at[t])
        for b in order:
            deliver_x(t, b)
        for b in order:
            deliver_z(t, b)
    for load in loads[2:]:
        load.wait()

    def softmax(b):
        drain(far_v.at[0, b, pl.ds(0, HALF - 1)], p2_recv.at[0, b])
        far_keys = far_v[0, b].reshape(PICKS * BLOCK, HEAD_SIZE)
        near_keys = ks_v[pl.ds(pl.multiple_of(b * BLOCK, BLOCK), BLOCK)]

        @pl.loop(0, GROUP)
        def _(h):
            for r in range(BLOCK // CHUNK):
                query = q_v[
                    pl.ds(pl.multiple_of(b * BLOCK + r * CHUNK, CHUNK), CHUNK),
                    pl.ds(pl.multiple_of(h * HEAD_SIZE, HEAD_SIZE), HEAD_SIZE),
                ]
                near = dot_rows(query, near_keys)
                below = (
                    r * CHUNK + lax.broadcasted_iota(jnp.int32, (CHUNK, BLOCK), 0)
                    >= lax.broadcasted_iota(jnp.int32, (CHUNK, BLOCK), 1)
                )
                near = jnp.where(below, near, -jnp.inf)
                far = dot_rows(query, far_keys)
                top = jnp.maximum(
                    jnp.max(near, axis=1, keepdims=True), jnp.max(far, axis=1, keepdims=True)
                )
                near = jnp.exp2((near - top) * LOG2_SCALE)
                far = jnp.exp2((far - top) * LOG2_SCALE)
                share = 1.0 / (
                    jnp.sum(near, axis=1, keepdims=True) + jnp.sum(far, axis=1, keepdims=True)
                )
                rows = pl.ds(r * CHUNK, CHUNK)
                weights_v[b, h, rows, 0:BLOCK] = (near * share).astype(jnp.bfloat16)
                weights_v[b, h, rows, BLOCK:LIST] = (far * share).astype(jnp.bfloat16)

    def give(t, h):
        rows = pl.ds(pl.multiple_of(t * OWN_ROWS, OWN_ROWS), OWN_ROWS)
        part = out_v.at[rows, pl.ds(pl.multiple_of(h * HEAD_SIZE, HEAD_SIZE), HEAD_SIZE)]
        at = pl.multiple_of((head * GROUP + h) * HEAD_SIZE, HEAD_SIZE)
        spot = out_ref.at[:, pl.ds(at, HEAD_SIZE)]

        @pl.when(t != head)
        def _():
            remote(part, spot, out_send.at[t], out_recv, "head", t).start()

        @pl.when(t == head)
        def _():
            pltpu.make_async_copy(part, spot, out_local).start()

    def combine(b):
        drain(far_v.at[1, b, pl.ds(0, HALF - 1)], p2_recv.at[1, b])
        far_values = far_v[1, b].reshape(PICKS * BLOCK, HEAD_SIZE)
        rows = pl.ds(pl.multiple_of(b * BLOCK, BLOCK), BLOCK)
        near_values = vs_v[rows]

        @pl.loop(0, GROUP)
        def _(h):
            total = jnp.dot(
                weights_v[b, h, :, 0:BLOCK], near_values, preferred_element_type=jnp.float32
            ) + jnp.dot(
                weights_v[b, h, :, BLOCK:LIST], far_values, preferred_element_type=jnp.float32
            )
            out_v[rows, pl.ds(pl.multiple_of(h * HEAD_SIZE, HEAD_SIZE), HEAD_SIZE)] = (
                total.astype(jnp.bfloat16)
            )
            for i in range(GROUP):
                give(b * GROUP + i, h)

    for b in order:
        softmax(b)
    for b in order:
        combine(b)
    drain(out_ref.at[:, pl.ds(0, (N_HEAD - 1) * GROUP * HEAD_SIZE)], out_recv)
    for t in range(N_HEAD):
        part = out_v.at[pl.ds(t * OWN_ROWS, OWN_ROWS)]

        @pl.when(t != head)
        def _():
            drain(part, out_send.at[t])

        @pl.when(t == head)
        def _():
            drain(part, out_local)

    drain(all_v.at[pl.ds(0, NZ - 1)], ch_send.at[0])
    drain(all_v.at[pl.ds(0, (NX - 1) * NZ)], ch_send.at[1])
    for t in range(2):
        drain(column_v.at[t, pl.ds(HOT, HOT * (NX - 1))], p1_send.at[t])
        drain(tables[t].at[pl.ds(0, HOT * NX * (NZ - 1))], p1_send.at[t])
        for b in range(Q_BLOCKS):
            drain(send_v.at[t, b], p2_send.at[t])
            drain(far_v.at[t, b, pl.ds(0, HALF - 1)], p2_send.at[t])


def shards(queries, span_keys, span_values, cached_keys, cached_values, chosen):
    rows, width = queries.shape
    bf16 = jnp.bfloat16
    anywhere = pl.BlockSpec(memory_space=pl.ANY)
    dma = pltpu.SemaphoreType.DMA
    return pl.pallas_call(
        kernel,
        out_shape=pltpu.VMEM((rows // N_HEAD, width * N_HEAD), bf16),
        in_specs=[anywhere] * 5 + [pl.BlockSpec(memory_space=pltpu.SMEM)],
        out_specs=pl.BlockSpec(memory_space=pltpu.VMEM),
        scratch_shapes=[
            pltpu.VMEM((rows, width), bf16),
            pltpu.VMEM((rows, HEAD_SIZE), bf16),
            pltpu.VMEM((rows, HEAD_SIZE), bf16),
            pltpu.VMEM((DEV_BLOCKS, BLOCK, HEAD_SIZE), bf16),
            pltpu.VMEM((DEV_BLOCKS, BLOCK, HEAD_SIZE), bf16),
            pltpu.VMEM((2, HOT, BLOCK, HEAD_SIZE), bf16),
            pltpu.VMEM((2, HOT * NX, COLUMN, HEAD_SIZE), bf16),
            pltpu.VMEM((HOT * N_CTX, ROWS, HEAD_SIZE), bf16),
            pltpu.VMEM((HOT * N_CTX, ROWS, HEAD_SIZE), bf16),
            pltpu.VMEM((2, Q_BLOCKS, NX - 1, HALF, PICKS * ROWS, HEAD_SIZE), bf16),
            pltpu.VMEM((2, Q_BLOCKS, NX, HALF, PICKS * ROWS, HEAD_SIZE), bf16),
            pltpu.VMEM((2, Q_BLOCKS, HALF, NX, PICKS * ROWS, HEAD_SIZE), bf16),
            pltpu.VMEM((1, 1, 128), jnp.int32),
            pltpu.VMEM((N_CTX, 1, 128), jnp.int32),
            pltpu.VMEM((N_CTX, 128), jnp.int32),
            pltpu.SMEM((N_CTX, 128), jnp.int32),
            pltpu.VMEM((Q_BLOCKS, GROUP, BLOCK, LIST), bf16),
            pltpu.VMEM((rows, width), bf16),
            dma((5,)), dma, dma((2,)), dma((2,)), dma((2,)), dma((2,)), dma((2,)), dma((2, 2)),
            dma((2,)), dma((2, 2)), dma((N_HEAD,)), dma, dma,
        ],
        compiler_params=pltpu.CompilerParams(
            collective_id=0, has_side_effects=True, vmem_limit_bytes=56 << 20
        ),
        cost_estimate=pl.CostEstimate(
            flops=4 * rows * GROUP * LIST * HEAD_SIZE,
            bytes_accessed=8 << 20,
            transcendentals=rows * GROUP * LIST,
        ),
    )(
        queries, span_keys, span_values,
        cached_keys.reshape(DEV_BLOCKS, BLOCK, HEAD_SIZE),
        cached_values.reshape(DEV_BLOCKS, BLOCK, HEAD_SIZE),
        chosen,
    )


def solution(mesh):
    placed = (P("ctx", "head"),) * 5 + (P("ctx", "head", None),)
    return jax.shard_map(
        shards, mesh=mesh, in_specs=placed, out_specs=P(("ctx", "head"), None), check_vma=False
    )
```

time: 124 us -> 117 us (0.944); the launches traced: 122 us -> 117 us
  Pallas kernels: 120 us -> 116 us
  local copies, waits for them, and re-layouts: 2.29 us -> 0.97 us
    pallas_call x1, Pallas kernels: 120 us -> 116 us  [shards(): pl.pallas_call(kernel, out_shape=pltpu.VMEM((rows // N_HEAD, width * N_HE...]
    unnamed x1, local copies, waits for them, and re-layouts: 2.29 us -> 0.97 us
where the time goes in v2:
time: 117 us
  Pallas kernels  116 us (99%)
    pallas_call x1, Pallas kernels, shards(): pl.pallas_call(kernel, out_shape=pltpu.VMEM((rows // N_HEAD, width * N_HE...  116 us

profile of v2, /device:TPU:1, one launch (start us, length us, event | category | flops | bytes accessed | tf_op | source)
XLA Modules:
  0.0 116.9 jit_solution(11644937285641905219)
XLA Ops:
  0.0 116.0 %shard_map.64 = bf16[128,4096]{1,0:T(8,128)(2,1)S(1)} custom-call(bf16[1024,512]{1,0:T(8,128)(2,1)} %q_hbm.1, bf16[1024,128]{1,0:T(8,128)(2,1)} %ks_hbm.1, bf16[1024,128]{1,0:T(8,128)(2,1)} %vs_hbm.1, bf16[8,512,128]{2,1,0:T(8,128)(2,1)} %bitcast.2, bf16[8,512,128]{2,1,0:T(8,128)(2,1)} %bitcast.3, s32[2,1,3]{2,1,0:T(1,128)} %chosen_ref.1), custom_call_target="tpu_custom_call" | custom-call | flops 4294967296 | bytes 8388608 | tf_op jit(solution)/shard_map/pallas_call | solution.py:339
  116.0 1.0 copy.8

commit v3 on v2

--- a/solution.py
+++ b/solution.py
@@ -54,9 +54,9 @@
 
 
 def kernel(
-    q_hbm, ks_hbm, vs_hbm, kc_hbm, vc_hbm, chosen_ref, out_ref,
+    q_hbm, ks_hbm, vs_hbm, kc_hbm, vc_hbm, chosen_hbm, out_ref,
     q_v, ks_v, vs_v, cache_k, cache_w, hot_v, column_v, table_k, table_w, send_v, relay_v, far_v,
-    row_v, all_v, index_v, index_s, weights_v, out_v,
+    chosen_s, row_v, all_v, index_v, index_s, weights_v, out_v,
     load_sem, index_sem, ch_send, ch_recv, p1_send, p1_recv, p2_send, p2_recv,
     x1_recv, x2_recv, out_send, out_recv, out_local,
 ):
@@ -71,6 +71,45 @@
 
     def along_z(d):
         return mx * NZ + (mz + d) % NZ
+
+    own = pltpu.make_async_copy(chosen_hbm, chosen_s, index_sem)
+    own.start()
+
+    def far_first(i):
+        return HALF + (i + 1) // 2 * (1 - i % 2 * 2)
+
+    barrier = pltpu.get_barrier_semaphore()
+
+    def greet(axis, peer):
+        pl.semaphore_signal(barrier, inc=1, device_id={axis: peer}, device_id_type=MESH)
+
+    @pl.loop(0, NZ - 1)
+    def _(i):
+        greet("ctx", along_z(far_first(i)))
+
+    for d in FAR_X:
+        greet("ctx", along_x(d))
+
+    @pl.loop(1, N_HEAD)
+    def _(i):
+        greet("head", (head + i) % N_HEAD)
+
+    own.wait()
+    lane = lax.broadcasted_iota(jnp.int32, (1, 128), 1)
+    mine = jnp.full((1, 128), -1, jnp.int32)
+    for b in range(Q_BLOCKS):
+        for j in range(PICKS):
+            mine = jnp.where(lane == b * PICKS + j, chosen_s[b, 0, j], mine)
+    row_v[0] = mine
+    all_v[me] = mine
+    pl.semaphore_wait(barrier, NZ - 1 + NX - 1 + N_HEAD - 1)
+
+    @pl.loop(0, NZ - 1)
+    def _(i):
+        remote(
+            row_v.at[0], all_v.at[me], ch_send.at[0], ch_recv.at[0], "ctx",
+            along_z(far_first(i)),
+        ).start()
 
     loads = [
         pltpu.make_async_copy(kc_hbm, cache_k, load_sem.at[0]),
@@ -81,41 +120,6 @@
     ]
     for load in loads[:2]:
         load.start()
-
-    def far_first(i):
-        return HALF + (i + 1) // 2 * (1 - i % 2 * 2)
-
-    barrier = pltpu.get_barrier_semaphore()
-
-    def greet(axis, peer):
-        pl.semaphore_signal(barrier, inc=1, device_id={axis: peer}, device_id_type=MESH)
-
-    @pl.loop(0, NZ - 1)
-    def _(i):
-        greet("ctx", along_z(far_first(i)))
-
-    for d in FAR_X:
-        greet("ctx", along_x(d))
-
-    @pl.loop(1, N_HEAD)
-    def _(i):
-        greet("head", (head + i) % N_HEAD)
-
-    lane = lax.broadcasted_iota(jnp.int32, (1, 128), 1)
-    mine = jnp.full((1, 128), -1, jnp.int32)
-    for b in range(Q_BLOCKS):
-        for j in range(PICKS):
-            mine = jnp.where(lane == b * PICKS + j, chosen_ref[b, 0, j], mine)
-    row_v[0] = mine
-    all_v[me] = mine
-    pl.semaphore_wait(barrier, NZ - 1 + NX - 1 + N_HEAD - 1)
-
-    @pl.loop(0, NZ - 1)
-    def _(i):
-        remote(
-            row_v.at[0], all_v.at[me], ch_send.at[0], ch_recv.at[0], "ctx",
-            along_z(far_first(i)),
-        ).start()
 
     drain(all_v.at[pl.ds(0, NZ - 1)], ch_recv.at[0])
     column = all_v.at[pl.ds(mx * NZ, NZ)]
@@ -148,13 +152,14 @@
         column_v[t, 0:HOT] = hot_v[t, :, pl.ds(at, COLUMN)]
 
     def spread_z(t, start, count):
-        @pl.loop(1, NZ)
+        @pl.loop(0, NZ - 1)
         def _(i):
-            at = pl.multiple_of((mz + i * 5) % HALF * ROWS, ROWS)
+            i = far_first(i)
+            at = pl.multiple_of((mz + i) % HALF * ROWS, ROWS)
             remote(
                 column_v.at[t, pl.ds(start, count), pl.ds(at, ROWS)],
                 tables[t].at[pl.ds(mz * HOT * NX + start, count)],
-                p1_send.at[t], p1_recv.at[t], "ctx", along_z(i * 5),
+                p1_send.at[t], p1_recv.at[t], "ctx", along_z(i),
             ).start()
 
         at = pl.multiple_of(mine_at * ROWS, ROWS)
@@ -234,10 +239,15 @@
     order = (lead, 1 - lead)
     for t in range(2):
         drain(tables[t].at[pl.ds(0, HOT * NX * (NZ - 1))], p1_recv.at[t])
-        for b in order:
-            deliver_x(t, b)
-        for b in order:
-            deliver_z(t, b)
+
+        @pl.loop(0, Q_BLOCKS)
+        def _(i):
+            deliver_x(t, (lead + i) % Q_BLOCKS)
+
+        @pl.loop(0, Q_BLOCKS)
+        def _(i):
+            deliver_z(t, (lead + i) % Q_BLOCKS)
+
     for load in loads[2:]:
         load.wait()
 
@@ -248,7 +258,8 @@
 
         @pl.loop(0, GROUP)
         def _(h):
-            for r in range(BLOCK // CHUNK):
+            @pl.loop(0, BLOCK // CHUNK)
+            def _(r):
                 query = q_v[
                     pl.ds(pl.multiple_of(b * BLOCK + r * CHUNK, CHUNK), CHUNK),
                     pl.ds(pl.multiple_of(h * HEAD_SIZE, HEAD_SIZE), HEAD_SIZE),
@@ -268,7 +279,7 @@
                 share = 1.0 / (
                     jnp.sum(near, axis=1, keepdims=True) + jnp.sum(far, axis=1, keepdims=True)
                 )
-                rows = pl.ds(r * CHUNK, CHUNK)
+                rows = pl.ds(pl.multiple_of(r * CHUNK, CHUNK), CHUNK)
                 weights_v[b, h, rows, 0:BLOCK] = (near * share).astype(jnp.bfloat16)
                 weights_v[b, h, rows, BLOCK:LIST] = (far * share).astype(jnp.bfloat16)
 
@@ -305,10 +316,14 @@
             for i in range(GROUP):
                 give(b * GROUP + i, h)
 
-    for b in order:
-        softmax(b)
-    for b in order:
-        combine(b)
+    @pl.loop(0, Q_BLOCKS)
+    def _(i):
+        softmax((lead + i) % Q_BLOCKS)
+
+    @pl.loop(0, Q_BLOCKS)
+    def _(i):
+        combine((lead + i) % Q_BLOCKS)
+
     drain(out_ref.at[:, pl.ds(0, (N_HEAD - 1) * GROUP * HEAD_SIZE)], out_recv)
     for t in range(N_HEAD):
         part = out_v.at[pl.ds(t * OWN_ROWS, OWN_ROWS)]
@@ -339,7 +354,7 @@
     return pl.pallas_call(
         kernel,
         out_shape=pltpu.VMEM((rows // N_HEAD, width * N_HEAD), bf16),
-        in_specs=[anywhere] * 5 + [pl.BlockSpec(memory_space=pltpu.SMEM)],
+        in_specs=[anywhere] * 6,
         out_specs=pl.BlockSpec(memory_space=pltpu.VMEM),
         scratch_shapes=[
             pltpu.VMEM((rows, width), bf16),
@@ -354,6 +369,7 @@
             pltpu.VMEM((2, Q_BLOCKS, NX - 1, HALF, PICKS * ROWS, HEAD_SIZE), bf16),
             pltpu.VMEM((2, Q_BLOCKS, NX, HALF, PICKS * ROWS, HEAD_SIZE), bf16),
             pltpu.VMEM((2, Q_BLOCKS, HALF, NX, PICKS * ROWS, HEAD_SIZE), bf16),
+            pltpu.SMEM(chosen.shape, jnp.int32),
             pltpu.VMEM((1, 1, 128), jnp.int32),
             pltpu.VMEM((N_CTX, 1, 128), jnp.int32),
             pltpu.VMEM((N_CTX, 128), jnp.int32),

time: 117 us -> 116 us (level)
  no operation moved by 1% of the time
where the time goes in v3:
time: 116 us
  Pallas kernels  115 us (99%)
    pallas_call x1, Pallas kernels, shards(): pl.pallas_call(kernel, out_shape=pltpu.VMEM((rows // N_HEAD, width * N_HE...  115 us

profile of v3, /device:TPU:1, one launch (start us, length us, event | category | flops | bytes accessed | tf_op | source)
XLA Modules:
  0.0 115.8 jit_solution(13161992186241274291)
XLA Ops:
  0.0 114.8 %shard_map.64 = bf16[128,4096]{1,0:T(8,128)(2,1)S(1)} custom-call(bf16[1024,512]{1,0:T(8,128)(2,1)} %q_hbm.1, bf16[1024,128]{1,0:T(8,128)(2,1)} %ks_hbm.1, bf16[1024,128]{1,0:T(8,128)(2,1)} %vs_hbm.1, bf16[8,512,128]{2,1,0:T(8,128)(2,1)} %bitcast.2, bf16[8,512,128]{2,1,0:T(8,128)(2,1)} %bitcast.3, s32[2,1,3]{2,1,0:T(1,128)} %chosen_hbm.1), custom_call_target="tpu_custom_call" | custom-call | flops 4294967296 | bytes 8388608 | tf_op jit(solution)/shard_map/pallas_call | solution.py:354
  114.8 1.0 copy.8
